TPU v7x, 32 devices: a whole 2x2x4 slice. The times are simulated.
32 devices in a mesh: groups: 2 (over x), expert: 8 (over z, y), dp: 2 (over core).
Axes of the slice: x: 2, y: 2, z: 4, core: 2. Of those that a mesh axis runs over, the one named last changes fastest.
Arguments:
- tokens: bfloat16 [1280, 4096], P(('groups', 'expert', 'dp')), parts along dimension 0, may hold values from -25 to 25
- routing: int32 [1280, 8], P(('groups', 'expert', 'dp')), parts along dimension 0, may hold values from 0 to 31, all different within a row; in each aligned block of 40 rows (0 to 39, 40 to 79, ...) at most 20 rows name the same one
- gate_weight: bfloat16 [32, 4096, 768], P('expert', 'dp'), may hold values from -0.09375 to 0.09375
- up_weight: bfloat16 [32, 4096, 768], P('expert', 'dp'), may hold values from -0.09375 to 0.09375
Outputs:
- input_gram: bfloat16 [2048, 64, 2048], P('dp', ('groups', 'expert')), parts along dimension 1
- hidden_gram: bfloat16 [768, 64, 768], P('dp', ('groups', 'expert')), parts along dimension 1
There are 2 independent parts, one for each index of `groups`. A program takes and returns all parts, laid end to end along the dimension named above; an argument that names none is the same for every part. Nothing has to cross between parts.
Inputs may be any that keep to these rules, and one draw needn't show every extreme that they name: `routing`: each row names 8 different experts. Among the rows of one device no expert is named by more than 20 rows.
All inputs are finite; a program needn't handle non-finite values.
Results may differ from a plain program's by a relative error of at most 0.01.
Values may be sent and summed in bfloat16 or wider, within the bound.
A program may use at most 256 MiB of HBM per device.

v0:
```python
import jax
import jax.numpy as jnp
from jax import lax
from jax.sharding import PartitionSpec as P

DW = 2048


def local(tokens, routing, gate_weight, up_weight):
    expert_count = lax.axis_size("expert")
    replica_count = lax.axis_size("dp")
    device_tokens = tokens.shape[0]
    local_experts = gate_weight.shape[0]
    experts_all = local_experts * expert_count
    capacity = device_tokens // 2
    factor = 2.0 / (device_tokens * expert_count * replica_count)
    labels = jnp.arange(experts_all, dtype=jnp.int32)
    chosen = jnp.any(routing[:, :, None] == labels[None, None, :], axis=1).astype(jnp.int32)
    before = jnp.cumsum(chosen, axis=0) - chosen
    slot_ids = jnp.arange(capacity, dtype=jnp.int32)
    placed = ((chosen[None, :, :] == 1) & (before[None, :, :] == slot_ids[:, None, None])).astype(
        jnp.bfloat16
    )
    outgoing = jnp.einsum("ctx,td->xcd", placed, tokens, preferred_element_type=jnp.float32).astype(
        jnp.bfloat16
    )
    arrived = lax.all_to_all(outgoing, "expert", split_axis=0, concat_axis=1, tiled=True)
    gate_part = jnp.einsum(
        "erd,edh->erh",
        arrived,
        lax.all_gather(gate_weight, "dp", axis=1, tiled=True),
        preferred_element_type=jnp.float32,
    )
    up_part = jnp.einsum(
        "erd,edh->erh",
        arrived,
        lax.all_gather(up_weight, "dp", axis=1, tiled=True),
        preferred_element_type=jnp.float32,
    )
    hidden = (jax.nn.silu(gate_part) * up_part).astype(jnp.bfloat16)
    window = arrived[:, :, :DW]
    row_block = window
    input_sum = lax.psum_scatter(
        jnp.einsum("erc,erj->cej", row_block, window, preferred_element_type=jnp.float32).astype(
            jnp.bfloat16
        ),
        "dp",
        scatter_dimension=0,
        tiled=True,
    ).astype(jnp.float32)
    row_block = hidden
    hidden_sum = lax.psum_scatter(
        jnp.einsum("erc,erj->cej", row_block, hidden, preferred_element_type=jnp.float32).astype(
            jnp.bfloat16
        ),
        "dp",
        scatter_dimension=0,
        tiled=True,
    ).astype(jnp.float32)
    return ((input_sum * factor).astype(jnp.bfloat16), (hidden_sum * factor).astype(jnp.bfloat16))


def solution(mesh):
    placed = (
        P(("groups", "expert", "dp"), None),
        P(("groups", "expert", "dp"), None),
        P("expert", "dp", None),
        P("expert", "dp", None),
    )
    return jax.shard_map(
        local,
        mesh=mesh,
        in_specs=placed,
        out_specs=(P("dp", ("groups", "expert"), None), P("dp", ("groups", "expert"), None)),
        check_vma=False,
    )
```

profile of v0, /device:TPU:0, one launch (start us, length us, event | category | flops | bytes accessed | tf_op | source)
XLA Modules:
  0.0 339.6 jit_solution(17814374451280888178)
XLA Ops:
  7.2 0.0 copy-start
  7.2 0.0 all-gather.3.cloned.1.call-start
  7.2 0.7 all-gather.3.cloned.1.call-update
  7.9 0.0 all-gather.5.cloned.1.call-start
  8.0 0.7 all-gather.5.cloned.1.call-update
  8.7 0.0 reduce-scatter.7.cloned.1.call-start
  8.8 0.1 copy.30
  8.9 0.1 reduce_window_sum.11
  8.9 0.1 copy.32
  9.0 0.1 copy.31
  9.1 0.0 copy-done
  9.1 1.5 fusion
  10.6 3.0 copy.33
  13.6 145.2 %all_to_all.18 = bf16[32,20,4096]{2,1,0:T(8,128)(2,1)S(1)} all-to-all(bf16[32,20,4096]{2,1,0:T(8,128)(2,1)S(1)} %copy.33), channel_id=1, replica_groups=mesh['groups'=2,'expert'=8,'dp'=2] {'expert'}, dimensions={0} | all-to-all | bytes 10485760 | tf_op jit(solution)/shard_map/all_to_all | solution.py:27
  158.8 6.5 %copy.34 = bf16[8,4,20,4096]{3,1,2,0:T(4,128)(2,1)} copy(bf16[8,4,20,4096]{3,2,1,0:T(8,128)(2,1)S(1)} %bitcast.18) | data formatting | bytes 10485760 | tf_op jit(solution)/shard_map/all_to_all | solution.py:27
  165.3 17.6 %fusion.12 = f32[4,160,768]{2,1,0:T(8,128)S(1)} fusion(bf16[4,4096,768]{2,1,0:T(8,128)(2,1)} %all-gather.3.cloned.1.call-done, bf16[4,160,4096]{2,0,1:T(4,128)(2,1)} %bitcast.19), kind=kOutput, calls=%fused_computation.20 | convolution fusion | flops 4026531840 | bytes 32374784 | tf_op jit(solution)/shard_map/erd,edh->erh/dot_general | solution.py:28
  182.9 0.0 all-gather.5.cloned.1.call-done
  182.9 34.7 %convolution_convert_fusion.1 = bf16[4,768,768]{2,1,0:T(8,128)(2,1)} fusion(f32[4,160,768]{2,1,0:T(8,128)S(1)} %fusion.12, bf16[4,4096,768]{2,1,0:T(8,128)(2,1)} %all-gather.5.cloned.1.call-done, bf16[4,160,4096]{2,0,1:T(4,128)(2,1)} %bitcast.20), kind=kOutput, calls=%fused_computation.5 | convolution fusion | flops 4786814976 | bytes 37093376 | tf_op jit(solution)/shard_map/erc,erj->cej/dot_general | solution.py:53
  217.6 6.6 %copy.42 = bf16[768,3072]{1,0:T(8,128)(2,1)} copy(bf16[768,3072]{0,1:T(8,128)(2,1)} %bitcast.23) | data formatting | bytes 9437184
  224.2 0.0 reduce-scatter.7.cloned.1.call-update
  224.2 0.0 reduce-scatter.5.cloned.1.call-start
  224.3 5.4 %copy.35 = bf16[4,160,4096]{2,1,0:T(8,128)(2,1)S(1)} copy(bf16[4,160,4096]{2,0,1:T(4,128)(2,1)} %bitcast.21) | data formatting | bytes 10485760 | tf_op jit(solution)/shard_map/all_to_all | solution.py:27
  229.7 14.6 %convert_bitcast_fusion = bf16[2048,4,2048]{0,2,1:T(8,128)(2,1)} fusion(bf16[4,160,4096]{2,1,0:T(8,128)(2,1)S(1)} %copy.35), kind=kOutput, calls=%fused_computation.1 | convolution fusion | flops 5385486336 | bytes 36175872 | tf_op jit(solution)/shard_map/erc,erj->cej/dot_general | solution.py:44
  244.2 0.0 reduce-scatter.5.cloned.1.call-update
  244.3 0.0 reduce-scatter.7.cloned.1.call-done
  244.3 3.0 copy.43
  247.3 1.9 multiply_convert_fusion.1
  249.2 5.6 %copy.39 = bf16[384,4,768]{2,1,0:T(4,128)(2,1)} copy(bf16[384,4,768]{0,2,1:T(8,128)(2,1)} %multiply_convert_fusion.1) | data formatting | bytes 4718592
  254.8 34.6 %reduce-scatter.5.cloned.1.call-done = bf16[1024,4,2048]{0,2,1:T(8,128)(2,1)} async-done(((bf16[2048,4,2048]{0,2,1:T(8,128)(2,1)}), bf16[1024,4,2048]{0,2,1:T(8,128)(2,1)}) %reduce-scatter.5.cloned.1.call-update) | async-done | bytes 16777232 | tf_op jit(solution)/shard_map/reduce_scatter | solution.py:43
  289.3 15.2 %multiply_convert_fusion = bf16[1024,4,2048]{0,2,1:T(8,128)(2,1)} fusion(bf16[1024,4,2048]{0,2,1:T(8,128)(2,1)} %reduce-scatter.5.cloned.1.call-done), kind=kLoop, calls=%fused_computation | loop fusion | flops 25165824 | bytes 33554432 | tf_op jit(solution)/shard_map/convert_element_type | solution.py:60
  304.5 28.5 %copy.38 = bf16[1024,4,2048]{2,1,0:T(4,128)(2,1)} copy(bf16[1024,4,2048]{0,2,1:T(8,128)(2,1)} %multiply_convert_fusion) | data formatting | bytes 33554432
  333.0 0.0 copy-done.1
  (7 shorter events, 0.1 us)
Async XLA Ops:
  7.2 1.9 copy-start
  7.2 158.1 %all-gather.3.cloned.1.call-start = ((), (), s32[]{:S(2)}) async-start(), calls=%async_computation.4 | async-start | bytes 37748736 | tf_op jit(solution)/shard_map/all_gather | solution.py:31
  7.9 0.8 copy-start.2
  7.9 175.0 %all-gather.5.cloned.1.call-start = ((), (), s32[]{:S(2)}) async-start(), calls=%async_computation.5 | async-start | bytes 37748736 | tf_op jit(solution)/shard_map/all_gather | solution.py:37
  8.7 235.6 %reduce-scatter.7.cloned.1.call-start = ((), (), s32[]{:S(2)}) async-start(), calls=%async_computation.6 | async-start | bytes 7077888
  224.2 65.1 %reduce-scatter.5.cloned.1.call-start = ((), (), s32[]{:S(2)}) async-start(), calls=%async_computation.3 | async-start | bytes 50331648 | tf_op jit(solution)/shard_map/reduce_scatter | solution.py:43
  304.5 28.5 %copy-start.1 = (bf16[40,4096]{1,0:T(8,128)(2,1)S(1)}, bf16[40,4096]{1,0:T(8,128)(2,1)}, u32[]{:S(2)}) copy-start(bf16[40,4096]{1,0:T(8,128)(2,1)} %param.4) | copy-start | bytes 983044
Sparse Core Ops, SparseCore 0:
  9.6 43.0 all-gather.2
  54.2 41.5 all-gather.4
  224.4 11.6 reduce-scatter.6
  244.4 44.9 reduce-scatter.4
where the time goes:
time: 341 us; the launch traced here: 340 us
  blocking collectives  145 us (43%)
  matrix products  68.4 us (20%)
  local copies, waits for them, and re-layouts  58.7 us (17%)
  waiting for transfers between devices  36 us (11%)
  other arithmetic  17.2 us (5%)
  between operations  13.8 us (4%)
    all_to_all x1, blocking collectives, local(): lax.all_to_all(outgoing, 'expert', split_axis=0, concat_axis=1, tiled=True)  145 us
    unnamed x10, local copies, waits for them, and re-layouts  43.7 us
    dot_general x1, matrix products, local(): jnp.einsum('erc,erj->cej', row_block, hidden, preferred_element_type=jnp....  34.7 us
    reduce_scatter x1, waiting for transfers between devices, local(): lax.psum_scatter(jnp.einsum('erc,erj->cej', row_block, window, preferred_...  34.6 us
    dot_general x1, matrix products, local(): jnp.einsum('erd,edh->erh', arrived, lax.all_gather(gate_weight, 'dp', axi...  17.6 us
    convert_element_type x1, other arithmetic, local(): (input_sum * factor).astype(jnp.bfloat16)  15.2 us
    dot_general x1, matrix products, local(): jnp.einsum('erc,erj->cej', row_block, window, preferred_element_type=jnp....  14.6 us
    all_to_all x2, local copies, waits for them, and re-layouts, local(): lax.all_to_all(outgoing, 'expert', split_axis=0, concat_axis=1, tiled=True)  11.8 us
  transfers between devices with their start and end apart: 4, of which 1 were waited for; matrix products, arithmetic and copies ran while one was open for 17% of the time, Pallas kernels for 0%

commit v1 on v0

v1 whole, which is shorter than its diff:
```python
import jax
import jax.numpy as jnp
from jax import lax
from jax.sharding import PartitionSpec as P

DW = 2048


def local(tokens, routing, gate_weight, up_weight):
    expert_count = lax.axis_size("expert")
    replica_count = lax.axis_size("dp")
    core = lax.axis_index("dp")
    device_tokens, topk = routing.shape
    local_experts, depth, hidden_width = gate_weight.shape
    factor = 2.0 / (device_tokens * expert_count * replica_count)
    swap = [(0, 1), (1, 0)]

    names = jnp.pad(routing.astype(jnp.bfloat16), ((0, 0), (0, 128 - topk)))
    own_cols = lax.dynamic_slice_in_dim(tokens, core * depth, depth, 1)
    other_cols = lax.dynamic_slice_in_dim(tokens, (1 - core) * depth, depth, 1)
    own_rows = jnp.concatenate([own_cols, names], axis=1)
    other_rows = lax.ppermute(jnp.concatenate([other_cols, names], axis=1), "dp", swap)

    labels = lax.axis_index("expert") * local_experts + jnp.arange(local_experts)

    def gathered(rows):
        got = lax.all_gather(rows, "expert", axis=0, tiled=True)
        x = got[:, :depth]
        named = got[:, depth : depth + topk].astype(jnp.int32)
        mask = jnp.any(named[None, :, :] == labels[:, None, None], axis=2)
        return x, mask, lax.ppermute(x[:, :DW], "dp", [(0, 1)])

    own_x, own_mask, sent_own = gathered(own_rows)
    other_x, other_mask, sent_other = gathered(other_rows)
    own_window = jnp.where(core == 0, own_x[:, :DW], sent_other)
    other_window = jnp.where(core == 0, other_x[:, :DW], sent_own)

    def project(x, w):
        return jnp.einsum("td,edh->eth", x, w, preferred_element_type=jnp.float32)

    other_gate = lax.ppermute(project(other_x, gate_weight).astype(jnp.bfloat16), "dp", swap)
    other_up = lax.ppermute(project(other_x, up_weight).astype(jnp.bfloat16), "dp", swap)
    gate = project(own_x, gate_weight) + other_gate.astype(jnp.float32)
    up = project(own_x, up_weight) + other_up.astype(jnp.float32)
    hidden = jnp.where(own_mask[:, :, None], jax.nn.silu(gate) * up, 0.0).astype(jnp.bfloat16)
    other_hidden = lax.ppermute(hidden, "dp", swap)

    window = jnp.concatenate([own_window, other_window], axis=0)
    mask = jnp.concatenate([own_mask, other_mask], axis=1)
    block = DW // replica_count
    rows = lax.dynamic_slice_in_dim(window, core * block, block, 1).T
    left = jnp.where(mask[None, :, :], rows[:, None, :], jnp.bfloat16(0))
    input_gram = jnp.einsum("iet,tj->iej", left, window, preferred_element_type=jnp.float32)

    hidden_all = jnp.concatenate([hidden, other_hidden], axis=1)
    h_block = hidden_width // replica_count
    h_rows = lax.dynamic_slice_in_dim(hidden_all, core * h_block, h_block, 2)
    hidden_gram = jnp.einsum("eti,etj->iej", h_rows, hidden_all, preferred_element_type=jnp.float32)
    return ((input_gram * factor).astype(jnp.bfloat16), (hidden_gram * factor).astype(jnp.bfloat16))


def solution(mesh):
    placed = (
        P(("groups", "expert", "dp"), None),
        P(("groups", "expert", "dp"), None),
        P("expert", "dp", None),
        P("expert", "dp", None),
    )
    return jax.shard_map(
        local,
        mesh=mesh,
        in_specs=placed,
        out_specs=(P("dp", ("groups", "expert"), None), P("dp", ("groups", "expert"), None)),
        check_vma=False,
    )
```

time: 341 us -> 216 us (0.63)
  blocking collectives: 145 us -> 0 us
  waiting for transfers between devices: 36 us -> 88.4 us
  other arithmetic: 17.2 us -> 2.13 us
  matrix products: 68.4 us -> 53.6 us
  local copies, waits for them, and re-layouts: 58.7 us -> 50.4 us
  starting transfers between devices: 0.16 us -> 7.35 us
    all_to_all x1 -> x0, blocking collectives: 145 us -> none  [local(): lax.all_to_all(outgoing, 'expert', split_axis=0, concat_axis=1, tiled=True)]
    all_gather x2, waiting for transfers between devices: 0.02 us -> 87.3 us  [gathered(): got = lax.all_gather(rows, 'expert', axis=0, tiled=True)]
    reduce_scatter x1 -> x0, waiting for transfers between devices: 34.6 us -> none  [local(): lax.psum_scatter(jnp.einsum('erc,erj->cej', row_block, window, preferred_...]
    convert_element_type x2 -> x3, other arithmetic: 17.1 us -> 0.71 us  [the longest x1 0.69 us: local(): names = jnp.pad(routing.astype(jnp.bfloat16), ((0, 0), (0, 128 - topk)))]
    dot_general x4 -> x6, matrix products: 68.4 us -> 53.6 us  [the longest x4 33.2 us: project(): return jnp.einsum('td,edh->eth', x, w, preferred_element_type=jnp.float32)]
    all_to_all x2 -> x0, local copies, waits for them, and re-layouts: 11.8 us -> none  [local(): lax.all_to_all(outgoing, 'expert', split_axis=0, concat_axis=1, tiled=True)]
    ppermute x0 -> x6, starting transfers between devices: none -> 7.27 us  [the longest x2 6.26 us: gathered(): return (x, mask, lax.ppermute(x[:, :DW], 'dp', [(0, 1)]))]
    slice x0 -> x4, local copies, waits for them, and re-layouts: none -> 3.57 us  [the longest x1 2.68 us: gathered(): x = got[:, :depth]]
  transfers between devices with their start and end apart: 4 -> 8, of which waited for: 1 -> 3; matrix products, arithmetic and copies ran while one was open for 17% -> 42% of each run, Pallas kernels for 0% -> 0%
where the time goes in v1:
time: 216 us
  waiting for transfers between devices  88.4 us (41%)
  matrix products  53.6 us (25%)
  local copies, waits for them, and re-layouts  50.4 us (23%)
  between operations  14.2 us (7%)
  starting transfers between devices  7.35 us (3%)
    all_gather x2, waiting for transfers between devices, gathered(): got = lax.all_gather(rows, 'expert', axis=0, tiled=True)  87.3 us
    unnamed x21, local copies, waits for them, and re-layouts  44.4 us
    dot_general x4, matrix products, project(): return jnp.einsum('td,edh->eth', x, w, preferred_element_type=jnp.float32)  33.2 us
    dot_general x1, matrix products, local(): jnp.einsum('iet,tj->iej', left, window, preferred_element_type=jnp.float32)  15.2 us
    ppermute x2, starting transfers between devices, gathered(): return (x, mask, lax.ppermute(x[:, :DW], 'dp', [(0, 1)]))  6.26 us
    dot_general x1, matrix products, local(): jnp.einsum('eti,etj->iej', h_rows, hidden_all, preferred_element_type=jnp...  5.17 us
  transfers between devices with their start and end apart: 8, of which 3 were waited for; matrix products, arithmetic and copies ran while one was open for 42% of the time, Pallas kernels for 0%

profile of v1, /device:TPU:0, one launch (start us, length us, event | category | flops | bytes accessed | tf_op | source)
XLA Modules:
  0.0 216.1 jit_solution(14715550173680056595)
XLA Ops:
  7.2 0.0 all-gather.3.cloned.1.call-start
  7.2 0.7 convert_element_type.41
  7.9 0.1 copy.39
  8.0 1.0 constant_dynamic-slice_fusion
  9.0 0.7 fusion.24
  9.7 0.0 all-gather.5.cloned.1.call-start
  9.8 0.5 collective-permute-start
  10.3 1.0 collective-permute-done
  11.4 0.7 copy-done.3
  12.1 44.2 %all-gather.3.cloned.1.call-done = bf16[320,2176]{1,0:T(8,128)(2,1)} async-done(((bf16[40,2176]{1,0:T(8,128)(2,1)}), bf16[320,2176]{1,0:T(8,128)(2,1)}) %all-gather.3.cloned.1.call-update) | async-done | bytes 1392656 | tf_op jit(solution)/shard_map/all_gather | solution.py:27
  56.3 0.9 slice.16
  57.2 0.1 copy.37
  57.3 43.1 %all-gather.5.cloned.1.call-done = bf16[320,2176]{1,0:T(8,128)(2,1)} async-done(((bf16[40,2176]{1,0:T(8,128)(2,1)}), bf16[320,2176]{1,0:T(8,128)(2,1)}) %all-gather.5.cloned.1.call-update) | async-done | bytes 1392656 | tf_op jit(solution)/shard_map/all_gather | solution.py:27
  100.4 2.7 %slice.19 = bf16[320,2048]{1,0:T(8,128)(2,1)} slice(bf16[320,2176]{1,0:T(8,128)(2,1)} %all-gather.5.cloned.1.call-done), slice={[0:320], [0:2048]} | slice | bytes 2621440 | tf_op jit(solution)/shard_map/slice | solution.py:28
  103.1 2.6 %collective-permute-start.1 = (bf16[320,2048]{1,0:T(8,128)(2,1)}, bf16[320,2048]{1,0:T(8,128)(2,1)}, u32[]{:S(2)}, u32[]{:S(2)}) collective-permute-start(bf16[320,2048]{1,0:T(8,128)(2,1)} %slice.19), channel_id=1, source_target_pairs={{0,1},{2,3},{4,5},{6,7},{8,9},{10,11},{12,13},{14,15},{16,17},{18,... | collective-permute-start | bytes 3932168 | tf_op jit(solution)/shard_map/ppermute | solution.py:31
  105.7 10.3 %convert_bitcast_fusion = bf16[4,320,768]{2,1,0:T(8,128)(2,1)} fusion(bf16[4,2048,768]{2,1,0:T(8,128)(2,1)} %param.7, bf16[320,2176]{1,0:T(8,128)(2,1)S(1)} %copy-done), kind=kOutput, calls=%fused_computation.21 | convolution fusion | flops 4027514880 | bytes 15859712 | tf_op jit(solution)/shard_map/td,edh->eth/dot_general | solution.py:39
  116.1 5.5 %convert_bitcast_fusion.1 = bf16[4,320,768]{2,1,0:T(8,128)(2,1)} fusion(bf16[4,2048,768]{2,1,0:T(8,128)(2,1)S(1)} %bitcast.38, bf16[320,2176]{1,0:T(8,128)(2,1)S(1)} %copy-done), kind=kOutput, calls=%fused_computation.22 | convolution fusion | flops 4027514880 | bytes 15859712 | tf_op jit(solution)/shard_map/td,edh->eth/dot_general | solution.py:39
  121.6 0.5 collective-permute-start.3
  122.1 6.2 %fusion.20 = f32[320,4,768]{2,0,1:T(8,128)} fusion(bf16[4,2048,768]{2,1,0:T(8,128)(2,1)S(1)} %bitcast.38, bf16[320,2176]{1,0:T(8,128)(2,1)S(1)} %copy-done.2), kind=kOutput, calls=%fused_computation.28 | convolution fusion | flops 4026531840 | bytes 17825792 | tf_op jit(solution)/shard_map/td,edh->eth/dot_general | solution.py:39
  128.3 0.1 copy.38
  128.4 0.1 compare_reduce_fusion.1
  128.5 0.1 pad_add_fusion
  128.6 0.2 broadcast_select_fusion.1
  128.8 3.6 %collective-permute-start.2 = (bf16[320,2048]{1,0:T(8,128)(2,1)S(1)}, bf16[320,2048]{1,0:T(8,128)(2,1)S(1)}, u32[]{:S(2)}, u32[]{:S(2)}) collective-permute-start(bf16[320,2048]{1,0:T(8,128)(2,1)S(1)} %get-tuple-element.13), channel_id=1, source_target_pairs={{0,1},{2,3},{4,5},{6,7},{8,9},{10,11},{12,13},{14,15},{16,17},{18,... | collective-permute-start | bytes 3932168 | tf_op jit(solution)/shard_map/ppermute | solution.py:31
  132.5 11.1 %fusion.5 = bf16[4,320,768]{2,1,0:T(8,128)(2,1)} fusion(bf16[4,320,768]{2,1,0:T(8,128)(2,1)} %collective-permute-done.4, f32[320,4,768]{2,0,1:T(8,128)S(1)} %copy-done.4, bf16[4,320,768]{2,1,0:T(8,128)(2,1)} %collective-permute-done.3, bf16[4,2048,768]{2,1,0:T(8,128)(2,1)} %param.7, pred[4,320]{1,0:T(4,128)(4,1)S(1)} %get-tuple-element.10, ...), kind=kOutput, calls=%fused_computation.11 | convolution fusion | flops 4037345280 | bytes 23725568 | tf_op jit(solution)/shard_map/td,edh->eth/dot_general | solution.py:39
  143.6 0.2 broadcast_select_fusion
  143.8 0.2 fusion.16
  144.0 1.4 copy.32
  145.4 15.2 %multiply_convert_fusion = bf16[1024,4,2048]{2,0,1:T(8,128)(2,1)S(1)} fusion(pred[4,640]{1,0:T(4,128)(4,1)S(1)} %pad_add_fusion, bf16[320,2048]{1,0:T(8,128)(2,1)S(1)} %broadcast_select_fusion, bf16[320,2048]{1,0:T(8,128)(2,1)} %copy-done.1, bf16[1024,640]{1,0:T(8,128)(2,1)} %copy.32), kind=kOutput, calls=%fused_computation | convolution fusion | flops 10762059776 | bytes 20711936 | tf_op jit(solution)/shard_map/iet,tj->iej/dot_general | solution.py:53
  160.6 40.1 %copy.34 = bf16[1024,4,2048]{2,1,0:T(4,128)(2,1)} copy(bf16[1024,4,2048]{2,0,1:T(8,128)(2,1)S(1)} %multiply_convert_fusion) | data formatting | bytes 33554432
  200.7 5.2 %fusion.10 = bf16[384,4,768]{0,2,1:T(8,128)(2,1)S(1)} fusion(s32[]{:T(128)S(6)} %select_n.40, bf16[4,320,768]{2,1,0:T(8,128)(2,1)} %fusion.5, bf16[4,320,768]{2,1,0:T(8,128)(2,1)} %collective-permute-done.5), kind=kOutput, calls=%fused_computation.19 | convolution fusion | flops 1524105216 | bytes 10223620 | tf_op jit(solution)/shard_map/eti,etj->iej/dot_general | solution.py:58
  205.9 3.4 %copy.35 = bf16[384,4,768]{2,1,0:T(4,128)(2,1)} copy(bf16[384,4,768]{0,2,1:T(8,128)(2,1)S(1)} %fusion.10) | data formatting | bytes 4718592
  (30 shorter events, 0.1 us)
Async XLA Ops:
  7.2 49.1 %all-gather.3.cloned.1.call-start = ((), (), s32[]{:S(2)}) async-start(), calls=%async_computation | async-start | bytes 1566720 | tf_op jit(solution)/shard_map/all_gather | solution.py:27
  9.7 90.6 %all-gather.5.cloned.1.call-start = ((), (), s32[]{:S(2)}) async-start(), calls=%async_computation.1 | async-start | bytes 1566720 | tf_op jit(solution)/shard_map/all_gather | solution.py:27
  9.8 1.6 collective-permute-start
  11.4 0.7 copy-start.3
  100.4 5.3 %copy-start = (bf16[320,2176]{1,0:T(8,128)(2,1)S(1)}, bf16[320,2176]{1,0:T(8,128)(2,1)}, u32[]{:S(2)}) copy-start(bf16[320,2176]{1,0:T(8,128)(2,1)} %all-gather.5.cloned.1.call-done) | copy-start | bytes 4177924
  100.4 15.6 %slice-start.1 = ((s8[12582912]{0:T(1024)(128)(4,1)}), s8[4194304]{0:T(1024)(128)(4,1)S(1)}, s32[]{:S(2)}) async-start(s8[12582912]{0:T(1024)(128)(4,1)} %bitcast.37), calls=%async_computation.3 | async-start | bytes 8388608
  103.1 13.0 %slice-start.2 = ((s8[12582912]{0:T(1024)(128)(4,1)}), s8[4194304]{0:T(1024)(128)(4,1)S(1)}, s32[]{:S(2)}) async-start(s8[12582912]{0:T(1024)(128)(4,1)} %bitcast.37), calls=%async_computation.4 | async-start | bytes 8388608
  103.1 13.0 %slice-start.3 = ((s8[12582912]{0:T(1024)(128)(4,1)}), s8[4194304]{0:T(1024)(128)(4,1)S(1)}, s32[]{:S(2)}) async-start(s8[12582912]{0:T(1024)(128)(4,1)} %bitcast.37), calls=%async_computation.5 | async-start | bytes 8388608
  103.1 25.5 %collective-permute-start.1 = (bf16[320,2048]{1,0:T(8,128)(2,1)}, bf16[320,2048]{1,0:T(8,128)(2,1)}, u32[]{:S(2)}, u32[]{:S(2)}) collective-permute-start(bf16[320,2048]{1,0:T(8,128)(2,1)} %slice.19), channel_id=1, source_target_pairs={{0,1},{2,3},{4,5},{6,7},{8,9},{10,11},{12,13},{14,15},{16,17},{18,... | collective-permute-start | bytes 3932168 | tf_op jit(solution)/shard_map/ppermute | solution.py:31
  116.0 6.1 %copy-start.2 = (bf16[320,2176]{1,0:T(8,128)(2,1)S(1)}, bf16[320,2176]{1,0:T(8,128)(2,1)}, u32[]{:S(2)}) copy-start(bf16[320,2176]{1,0:T(8,128)(2,1)} %all-gather.3.cloned.1.call-done) | copy-start | bytes 4177924
  116.0 16.4 %collective-permute-start.4 = (bf16[4,320,768]{2,1,0:T(8,128)(2,1)}, bf16[4,320,768]{2,1,0:T(8,128)(2,1)}, u32[]{:S(2)}, u32[]{:S(2)}) collective-permute-start(bf16[4,320,768]{2,1,0:T(8,128)(2,1)} %convert_bitcast_fusion), channel_id=1, source_target_pairs={{0,1},{1,0},{2,3},{3,2},{4,5},{5,4},{6,7},{7,6},{8,9},{9,8},{10,11... | collective-permute-start | bytes 5898248 | tf_op jit(solution)/shard_map/ppermute | solution.py:42
  121.6 6.7 %slice-start = ((bf16[320,2176]{1,0:T(8,128)(2,1)}), bf16[320,8]{1,0:T(8,128)(2,1)S(1)}, s32[]{:S(2)}) async-start(bf16[320,2176]{1,0:T(8,128)(2,1)} %all-gather.5.cloned.1.call-done), calls=%async_computation.2 | async-start | bytes 163840 | tf_op jit(solution)/shard_map/slice | solution.py:29
  121.6 10.9 %collective-permute-start.3 = (bf16[4,320,768]{2,1,0:T(8,128)(2,1)}, bf16[4,320,768]{2,1,0:T(8,128)(2,1)}, u32[]{:S(2)}, u32[]{:S(2)}) collective-permute-start(bf16[4,320,768]{2,1,0:T(8,128)(2,1)} %convert_bitcast_fusion.1), channel_id=1, source_target_pairs={{0,1},{1,0},{2,3},{3,2},{4,5},{5,4},{6,7},{7,6},{8,9},{9,8},{10,11... | collective-permute-start | bytes 5898248 | tf_op jit(solution)/shard_map/ppermute | solution.py:41
  128.6 3.9 %copy-start.4 = (f32[320,4,768]{2,0,1:T(8,128)S(1)}, f32[320,4,768]{2,0,1:T(8,128)}, u32[]{:S(2)}) copy-start(f32[320,4,768]{2,0,1:T(8,128)} %fusion.20) | copy-start | bytes 11796484
  128.8 15.0 %copy-start.1 = (bf16[320,2048]{1,0:T(8,128)(2,1)}, bf16[320,2048]{1,0:T(8,128)(2,1)S(1)}, u32[]{:S(2)}) copy-start(bf16[320,2048]{1,0:T(8,128)(2,1)S(1)} %get-tuple-element.12) | copy-start | bytes 3932164
  128.8 14.8 %collective-permute-start.2 = (bf16[320,2048]{1,0:T(8,128)(2,1)S(1)}, bf16[320,2048]{1,0:T(8,128)(2,1)S(1)}, u32[]{:S(2)}, u32[]{:S(2)}) collective-permute-start(bf16[320,2048]{1,0:T(8,128)(2,1)S(1)} %get-tuple-element.13), channel_id=1, source_target_pairs={{0,1},{2,3},{4,5},{6,7},{8,9},{10,11},{12,13},{14,15},{16,17},{18,... | collective-permute-start | bytes 3932168 | tf_op jit(solution)/shard_map/ppermute | solution.py:31
  143.6 57.1 %collective-permute-start.5 = (bf16[4,320,768]{2,1,0:T(8,128)(2,1)}, bf16[4,320,768]{2,1,0:T(8,128)(2,1)}, u32[]{:S(2)}, u32[]{:S(2)}) collective-permute-start(bf16[4,320,768]{2,1,0:T(8,128)(2,1)} %fusion.5), channel_id=1, source_target_pairs={{0,1},{1,0},{2,3},{3,2},{4,5},{5,4},{6,7},{7,6},{8,9},{9,8},{10,11... | collective-permute-start | bytes 5898248 | tf_op jit(solution)/shard_map/ppermute | solution.py:46
Sparse Core Ops, SparseCore 0:
  10.8 45.4 all-gather.2
  59.1 41.2 all-gather.4

commit v2 on v1

--- a/solution.py
+++ b/solution.py
@@ -1,9 +1,92 @@
+import functools
+
 import jax
 import jax.numpy as jnp
 from jax import lax
+from jax.experimental import pallas as pl
+from jax.experimental.pallas import tpu as pltpu
 from jax.sharding import PartitionSpec as P
 
 DW = 2048
+ROW_PAD = 16
+MESH = pl.DeviceIdType.MESH
+
+
+def gather_kernel(experts, cores, rows_ref, out_ref, send_sem, recv_sem, own_sem):
+    expert, core = lax.axis_index("expert"), lax.axis_index("dp")
+    number = experts * cores
+    me = expert * cores + core
+
+    def peer(step):
+        index = lax.rem(me + step, number)
+        return {"expert": index // cores, "dp": lax.rem(index, cores)}
+
+    barrier = pltpu.get_barrier_semaphore()
+    for step in range(1, number):
+        pl.semaphore_signal(barrier, inc=1, device_id=peer(step), device_id_type=MESH)
+    pl.semaphore_wait(barrier, number - 1)
+    copies = []
+    for step in range(1, number):
+        target = peer(step)
+        copy = pltpu.make_async_remote_copy(
+            src_ref=rows_ref.at[target["dp"]],
+            dst_ref=out_ref.at[lax.rem(core + target["dp"], cores), expert],
+            send_sem=send_sem.at[step],
+            recv_sem=recv_sem.at[step],
+            device_id=target,
+            device_id_type=MESH,
+        )
+        copy.start()
+        copies.append(copy)
+    own = pltpu.make_async_copy(rows_ref.at[core], out_ref.at[0, expert], own_sem)
+    own.start()
+    own.wait()
+    for copy in copies:
+        copy.wait()
+
+
+def gather(rows, experts):
+    cores = rows.shape[0]
+    number = experts * cores
+    return pl.pallas_call(
+        functools.partial(gather_kernel, experts, cores),
+        out_shape=jax.ShapeDtypeStruct((cores, experts) + rows.shape[1:], rows.dtype),
+        in_specs=[pl.BlockSpec(memory_space=pl.ANY)],
+        out_specs=pl.BlockSpec(memory_space=pl.ANY),
+        scratch_shapes=[
+            pltpu.SemaphoreType.DMA((number,)),
+            pltpu.SemaphoreType.DMA((number,)),
+            pltpu.SemaphoreType.DMA,
+        ],
+        compiler_params=pltpu.CompilerParams(collective_id=0, has_side_effects=True),
+    )(rows)
+
+
+def gram_kernel(factor, left_ref, right_ref, out_ref):
+    total = jnp.dot(left_ref[...], right_ref[...], preferred_element_type=jnp.float32)
+    out_ref[...] = (total * factor).reshape(out_ref.shape).astype(out_ref.dtype)
+
+
+def gram(left, right, experts, factor):
+    rows, depth = left.shape
+    width = right.shape[1]
+    tile = min(64, rows // experts)
+    return pl.pallas_call(
+        functools.partial(gram_kernel, factor),
+        out_shape=jax.ShapeDtypeStruct((rows // experts, experts, width), jnp.bfloat16),
+        grid=(rows // experts // tile,),
+        in_specs=[
+            pl.BlockSpec((tile * experts, depth), lambda i: (i, 0)),
+            pl.BlockSpec((depth, width), lambda i: (0, 0)),
+        ],
+        out_specs=pl.BlockSpec((tile, experts, width), lambda i: (i, 0, 0)),
+        compiler_params=pltpu.CompilerParams(vmem_limit_bytes=40 << 20),
+        cost_estimate=pl.CostEstimate(
+            flops=2 * rows * depth * width,
+            bytes_accessed=2 * (rows * depth + depth * width + rows * width),
+            transcendentals=0,
+        ),
+    )(left, right)
 
 
 def local(tokens, routing, gate_weight, up_weight):
@@ -15,23 +98,30 @@
     factor = 2.0 / (device_tokens * expert_count * replica_count)
     swap = [(0, 1), (1, 0)]
 
-    names = jnp.pad(routing.astype(jnp.bfloat16), ((0, 0), (0, 128 - topk)))
-    own_cols = lax.dynamic_slice_in_dim(tokens, core * depth, depth, 1)
-    other_cols = lax.dynamic_slice_in_dim(tokens, (1 - core) * depth, depth, 1)
-    own_rows = jnp.concatenate([own_cols, names], axis=1)
-    other_rows = lax.ppermute(jnp.concatenate([other_cols, names], axis=1), "dp", swap)
+    row_count = -(-device_tokens // ROW_PAD) * ROW_PAD
+    extra = ((0, row_count - device_tokens), (0, 0))
+    names = jnp.pad(routing, extra, constant_values=-1)
+    names = jnp.pad(names, ((0, 0), (0, 128 - topk))).astype(jnp.bfloat16)
+    padded = jnp.pad(tokens, extra)
+    rows = jnp.stack(
+        [
+            jnp.concatenate([padded[:, c * depth : (c + 1) * depth], names], axis=1)
+            for c in range(replica_count)
+        ]
+    )
+    gathered_rows = gather(rows, expert_count)
 
     labels = lax.axis_index("expert") * local_experts + jnp.arange(local_experts)
 
-    def gathered(rows):
-        got = lax.all_gather(rows, "expert", axis=0, tiled=True)
+    def gathered(got):
+        got = got.reshape(expert_count * row_count, got.shape[-1])
         x = got[:, :depth]
         named = got[:, depth : depth + topk].astype(jnp.int32)
         mask = jnp.any(named[None, :, :] == labels[:, None, None], axis=2)
         return x, mask, lax.ppermute(x[:, :DW], "dp", [(0, 1)])
 
-    own_x, own_mask, sent_own = gathered(own_rows)
-    other_x, other_mask, sent_other = gathered(other_rows)
+    own_x, own_mask, sent_own = gathered(gathered_rows[0])
+    other_x, other_mask, sent_other = gathered(gathered_rows[1])
     own_window = jnp.where(core == 0, own_x[:, :DW], sent_other)
     other_window = jnp.where(core == 0, other_x[:, :DW], sent_own)
 
@@ -49,14 +139,16 @@
     mask = jnp.concatenate([own_mask, other_mask], axis=1)
     block = DW // replica_count
     rows = lax.dynamic_slice_in_dim(window, core * block, block, 1).T
-    left = jnp.where(mask[None, :, :], rows[:, None, :], jnp.bfloat16(0))
-    input_gram = jnp.einsum("iet,tj->iej", left, window, preferred_element_type=jnp.float32)
+    left = jnp.where(
+        jnp.tile(mask, (block, 1)), jnp.repeat(rows, local_experts, axis=0), jnp.bfloat16(0)
+    )
+    input_gram = gram(left, window, local_experts, factor)
 
     hidden_all = jnp.concatenate([hidden, other_hidden], axis=1)
     h_block = hidden_width // replica_count
     h_rows = lax.dynamic_slice_in_dim(hidden_all, core * h_block, h_block, 2)
     hidden_gram = jnp.einsum("eti,etj->iej", h_rows, hidden_all, preferred_element_type=jnp.float32)
-    return ((input_gram * factor).astype(jnp.bfloat16), (hidden_gram * factor).astype(jnp.bfloat16))
+    return (input_gram, (hidden_gram * factor).astype(jnp.bfloat16))
 
 
 def solution(mesh):

time: 216 us -> 188 us (0.87)
  the two profiles are of different devices: /device:TPU:0 before, /device:TPU:13 now
where the time goes in v2:
time: 188 us; the launch traced here: 187 us
  Pallas kernels  96.5 us (51%)
  matrix products  44.4 us (24%)
  local copies, waits for them, and re-layouts  26.7 us (14%)
  other arithmetic  12.3 us (7%)
  starting transfers between devices  6.35 us (3%)
    pallas_call x1, Pallas kernels, gather(): pl.pallas_call(functools.partial(gather_kernel, experts, cores), out_shap...  77.4 us
    dot_general x4, matrix products, project(): return jnp.einsum('td,edh->eth', x, w, preferred_element_type=jnp.float32)  37.3 us
    pallas_call x1, Pallas kernels, gram(): pl.pallas_call(functools.partial(gram_kernel, factor), out_shape=jax.Shap...  19.2 us
    select_n x1, local copies, waits for them, and re-layouts, local(): jnp.where(jnp.tile(mask, (block, 1)), jnp.repeat(rows, local_experts, axi...  10.9 us
    unnamed x13, local copies, waits for them, and re-layouts  7.8 us
    dot_general x1, matrix products, local(): jnp.einsum('eti,etj->iej', h_rows, hidden_all, preferred_element_type=jnp...  7.13 us
    select_n x1, other arithmetic, local(): jnp.where(jnp.tile(mask, (block, 1)), jnp.repeat(rows, local_experts, axi...  6.84 us
  transfers between devices with their start and end apart: 5, of which 0 were waited for; matrix products, arithmetic and copies ran while one was open for 33% of the time, Pallas kernels for 10%

profile of v2, /device:TPU:13, one launch (start us, length us, event | category | flops | bytes accessed | tf_op | source)
XLA Modules:
  0.0 187.1 jit_solution(17913379541249869713)
XLA Ops:
  0.6 0.7 convert.6
  1.3 0.1 copy.16
  1.4 1.0 pad_slice_fusion.1
  2.5 0.8 pad_maximum_fusion.5.rows_ref
  3.3 77.4 %shard_map.59 = bf16[2,8,48,2176]{3,2,1,0:T(8,128)(2,1)} custom-call(bf16[2,48,2176]{2,1,0:T(8,128)(2,1)} %pad_maximum_fusion.5.rows_ref), custom_call_target="tpu_custom_call" | custom-call | tf_op jit(solution)/shard_map/pallas_call | solution.py:51
  80.7 2.2 %fusion.25 = (bf16[1,8,48,2176]{3,2,1,0:T(8,128)(2,1)S(1)}, bf16[1,8,48,2176]{3,2,1,0:T(8,128)(2,1)S(1)}) fusion(bf16[2,8,48,2176]{3,2,1,0:T(8,128)(2,1)} %shard_map.59), kind=kLoop, calls=%fused_computation.48 | loop fusion | bytes 6684672 | tf_op jit(solution)/shard_map/slice | solution.py:124
  82.9 1.4 slice.34
  84.2 1.4 collective-permute-start.1
  85.7 0.0 slice-start.1
  85.7 11.0 %convert_bitcast_fusion = bf16[4,384,768]{2,1,0:T(8,128)(2,1)} fusion(bf16[4,2048,768]{2,1,0:T(8,128)(2,1)} %param.7, bf16[384,2176]{1,0:T(8,128)(2,1)S(1)} %bitcast.45), kind=kOutput, calls=%fused_computation.16 | convolution fusion | flops 4833017856 | bytes 16515072 | tf_op jit(solution)/shard_map/td,edh->eth/dot_general | solution.py:129
  96.7 2.2 %collective-permute-start.3 = (bf16[4,384,768]{2,1,0:T(8,128)(2,1)}, bf16[4,384,768]{2,1,0:T(8,128)(2,1)}, u32[]{:S(2)}, u32[]{:S(2)}) collective-permute-start(bf16[4,384,768]{2,1,0:T(8,128)(2,1)} %convert_bitcast_fusion), channel_id=1, source_target_pairs={{0,1},{1,0},{2,3},{3,2},{4,5},{5,4},{6,7},{7,6},{8,9},{9,8},{10,11... | collective-permute-start | bytes 7077896 | tf_op jit(solution)/shard_map/ppermute | solution.py:132
  98.9 6.3 %convert_bitcast_fusion.1 = bf16[4,384,768]{2,1,0:T(8,128)(2,1)} fusion(bf16[4,2048,768]{2,1,0:T(8,128)(2,1)S(1)} %bitcast.50, bf16[384,2176]{1,0:T(8,128)(2,1)S(1)} %bitcast.46), kind=kOutput, calls=%fused_computation.17 | convolution fusion | flops 4833017856 | bytes 16515072 | tf_op jit(solution)/shard_map/td,edh->eth/dot_general | solution.py:129
  105.2 0.0 collective-permute-start.2
  105.2 0.7 slice_convert_fusion
  106.0 1.0 copy.18
  107.0 0.7 copy.17
  107.7 0.8 compare_reduce_fusion.1
  108.5 8.1 %fusion.12 = f32[384,4,768]{2,0,1:T(8,128)S(1)} fusion(bf16[4,2048,768]{2,1,0:T(8,128)(2,1)} %param.6, bf16[384,2176]{1,0:T(8,128)(2,1)S(1)} %bitcast.42), kind=kOutput, calls=%fused_computation.23 | convolution fusion | flops 4831838208 | bytes 18874368 | tf_op jit(solution)/shard_map/td,edh->eth/dot_general | solution.py:129
  116.6 1.6 broadcast_select_fusion.1
  118.3 1.5 collective-permute-start
  119.8 11.9 %fusion.3 = bf16[4,384,768]{2,1,0:T(8,128)(2,1)} fusion(bf16[4,384,768]{2,1,0:T(8,128)(2,1)} %collective-permute-done.3, f32[384,4,768]{2,0,1:T(8,128)S(1)} %fusion.12, bf16[4,384,768]{2,1,0:T(8,128)(2,1)} %collective-permute-done.2, pred[4,384]{1,0:T(4,128)(4,1)S(1)} %get-tuple-element.8, bf16[4,2048,768]{2,1,0:T(8,128)(2,1)} %param.7, ...), kind=kOutput, calls=%fused_computation.8 | convolution fusion | flops 4844814336 | bytes 25953792 | tf_op jit(solution)/shard_map/td,edh->eth/dot_general | solution.py:129
  131.7 1.2 collective-permute-start.4
  132.9 0.2 broadcast_select_fusion.2
  133.1 0.2 fusion.8
  133.3 1.6 copy.19
  134.9 6.8 %broadcast_select_fusion = bf16[1024,4,768]{2,1,0:T(4,128)(2,1)} fusion(pred[4,768]{1,0:T(4,128)(4,1)S(1)} %pad_add_fusion, bf16[1024,768]{1,0:T(8,128)(2,1)} %copy.19), kind=kLoop, calls=%fused_computation | loop fusion | flops 3145728 | bytes 7867392 | tf_op jit(solution)/shard_map/jit(_where)/select_n | solution.py:142
  141.8 10.9 %select_n.33.left_ref = bf16[4096,768]{1,0:T(8,128)(2,1)} reshape(bf16[1024,4,768]{2,1,0:T(4,128)(2,1)} %broadcast_select_fusion) | data formatting | bytes 12582912 | tf_op jit(solution)/shard_map/jit(_where)/select_n | solution.py:142
  152.6 0.4 pad_maximum_fusion.2.right_ref
  153.0 2.4 %copy-done = bf16[4096,768]{1,0:T(8,128)(2,1)S(1)} copy-done((bf16[4096,768]{1,0:T(8,128)(2,1)S(1)}, bf16[4096,768]{1,0:T(8,128)(2,1)}, u32[]{:S(2)}) %copy-start) | copy-done | bytes 6291480
  155.4 19.2 %shard_map.60 = bf16[1024,4,2048]{2,1,0:T(4,128)(2,1)} custom-call(bf16[4096,768]{1,0:T(8,128)(2,1)S(1)} %copy-done, bf16[768,2048]{1,0:T(8,128)(2,1)S(1)} %pad_maximum_fusion.2.right_ref), custom_call_target="tpu_custom_call" | custom-call | flops 12884901888 | bytes 26214400 | tf_op jit(solution)/shard_map/pallas_call | solution.py:74
  174.6 7.1 %fusion.4 = bf16[384,4,768]{0,2,1:T(8,128)(2,1)} fusion(s32[]{:T(128)S(6)} %select_n.35, bf16[4,384,768]{2,1,0:T(8,128)(2,1)} %fusion.3, bf16[4,384,768]{2,1,0:T(8,128)(2,1)} %collective-permute-done.4), kind=kOutput, calls=%fused_computation.14 | convolution fusion | flops 1828454400 | bytes 11796484 | tf_op jit(solution)/shard_map/eti,etj->iej/dot_general | solution.py:150
  181.7 5.4 %copy.21 = bf16[384,4,768]{2,1,0:T(4,128)(2,1)} copy(bf16[384,4,768]{0,2,1:T(8,128)(2,1)} %fusion.4) | data formatting | bytes 4718592
  (21 shorter events, 0.1 us)
Async XLA Ops:
  82.8 16.1 %slice-start = ((s8[12582912]{0:T(1024)(128)(4,1)}), s8[4194304]{0:T(1024)(128)(4,1)S(1)}, s32[]{:S(2)}) async-start(s8[12582912]{0:T(1024)(128)(4,1)} %bitcast.49), calls=%async_computation | async-start | bytes 8388608
  84.2 32.4 %collective-permute-start.1 = (bf16[384,2048]{1,0:T(8,128)(2,1)}, bf16[384,2048]{1,0:T(8,128)(2,1)}, u32[]{:S(2)}, u32[]{:S(2)}) collective-permute-start(bf16[384,2048]{1,0:T(8,128)(2,1)} %slice.34), channel_id=1, source_target_pairs={{0,1},{2,3},{4,5},{6,7},{8,9},{10,11},{12,13},{14,15},{16,17},{18,... | collective-permute-start | bytes 4718600 | tf_op jit(solution)/shard_map/ppermute | solution.py:121
  85.7 13.2 %slice-start.1 = ((s8[12582912]{0:T(1024)(128)(4,1)}), s8[4194304]{0:T(1024)(128)(4,1)S(1)}, s32[]{:S(2)}) async-start(s8[12582912]{0:T(1024)(128)(4,1)} %bitcast.49), calls=%async_computation.1 | async-start | bytes 8388608
  85.7 13.2 %slice-start.2 = ((s8[12582912]{0:T(1024)(128)(4,1)}), s8[4194304]{0:T(1024)(128)(4,1)S(1)}, s32[]{:S(2)}) async-start(s8[12582912]{0:T(1024)(128)(4,1)} %bitcast.49), calls=%async_computation.2 | async-start | bytes 8388608
  96.7 23.1 %collective-permute-start.3 = (bf16[4,384,768]{2,1,0:T(8,128)(2,1)}, bf16[4,384,768]{2,1,0:T(8,128)(2,1)}, u32[]{:S(2)}, u32[]{:S(2)}) collective-permute-start(bf16[4,384,768]{2,1,0:T(8,128)(2,1)} %convert_bitcast_fusion), channel_id=1, source_target_pairs={{0,1},{1,0},{2,3},{3,2},{4,5},{5,4},{6,7},{7,6},{8,9},{9,8},{10,11... | collective-permute-start | bytes 7077896 | tf_op jit(solution)/shard_map/ppermute | solution.py:132
  105.2 14.5 %collective-permute-start.2 = (bf16[4,384,768]{2,1,0:T(8,128)(2,1)}, bf16[4,384,768]{2,1,0:T(8,128)(2,1)}, u32[]{:S(2)}, u32[]{:S(2)}) collective-permute-start(bf16[4,384,768]{2,1,0:T(8,128)(2,1)} %convert_bitcast_fusion.1), channel_id=1, source_target_pairs={{0,1},{1,0},{2,3},{3,2},{4,5},{5,4},{6,7},{7,6},{8,9},{9,8},{10,11... | collective-permute-start | bytes 7077896 | tf_op jit(solution)/shard_map/ppermute | solution.py:131
  118.2 14.9 %copy-start.1 = (bf16[384,2048]{1,0:T(8,128)(2,1)}, bf16[384,2048]{1,0:T(8,128)(2,1)S(1)}, u32[]{:S(2)}) copy-start(bf16[384,2048]{1,0:T(8,128)(2,1)S(1)} %get-tuple-element.12) | copy-start | bytes 4718596
  118.3 14.7 %collective-permute-start = (bf16[384,2048]{1,0:T(8,128)(2,1)S(1)}, bf16[384,2048]{1,0:T(8,128)(2,1)S(1)}, u32[]{:S(2)}, u32[]{:S(2)}) collective-permute-start(bf16[384,2048]{1,0:T(8,128)(2,1)S(1)} %get-tuple-element.13), channel_id=1, source_target_pairs={{0,1},{2,3},{4,5},{6,7},{8,9},{10,11},{12,13},{14,15},{16,17},{18,... | collective-permute-start | bytes 4718600 | tf_op jit(solution)/shard_map/ppermute | solution.py:121
  131.7 42.9 %collective-permute-start.4 = (bf16[4,384,768]{2,1,0:T(8,128)(2,1)}, bf16[4,384,768]{2,1,0:T(8,128)(2,1)}, u32[]{:S(2)}, u32[]{:S(2)}) collective-permute-start(bf16[4,384,768]{2,1,0:T(8,128)(2,1)} %fusion.3), channel_id=1, source_target_pairs={{0,1},{1,0},{2,3},{3,2},{4,5},{5,4},{6,7},{7,6},{8,9},{9,8},{10,11... | collective-permute-start | bytes 7077896 | tf_op jit(solution)/shard_map/ppermute | solution.py:136
  141.8 10.9 %copy-start.2 = (bf16[384,2048]{1,0:T(8,128)(2,1)S(1)}, bf16[384,2048]{1,0:T(8,128)(2,1)}, u32[]{:S(2)}) copy-start(bf16[384,2048]{1,0:T(8,128)(2,1)} %copy-done.1) | copy-start | bytes 4718596
  152.6 2.8 %copy-start = (bf16[4096,768]{1,0:T(8,128)(2,1)S(1)}, bf16[4096,768]{1,0:T(8,128)(2,1)}, u32[]{:S(2)}) copy-start(bf16[4096,768]{1,0:T(8,128)(2,1)} %select_n.33.left_ref) | copy-start | bytes 18874372

commit v3 on v2

--- a/solution.py
+++ b/solution.py
@@ -12,81 +12,117 @@
 MESH = pl.DeviceIdType.MESH
 
 
-def gather_kernel(experts, cores, rows_ref, out_ref, send_sem, recv_sem, own_sem):
+def gather_kernel(experts, cores, rows_ref, out_ref, swap_sem, send_sem, recv_sem, own_sem):
     expert, core = lax.axis_index("expert"), lax.axis_index("dp")
-    number = experts * cores
-    me = expert * cores + core
-
-    def peer(step):
-        index = lax.rem(me + step, number)
-        return {"expert": index // cores, "dp": lax.rem(index, cores)}
+    other = {"dp": 1 - core}
+
+    def index_at(place):
+        place = lax.rem(place + 2 * experts, experts)
+        return jnp.where(2 * place < experts, 2 * place, 2 * (experts - 1 - place) + 1)
+
+    half = expert // 2
+    me = jnp.where(lax.rem(expert, 2) == 0, half, experts - 1 - half)
+    ways = (1, -1)
 
     barrier = pltpu.get_barrier_semaphore()
-    for step in range(1, number):
-        pl.semaphore_signal(barrier, inc=1, device_id=peer(step), device_id_type=MESH)
-    pl.semaphore_wait(barrier, number - 1)
-    copies = []
-    for step in range(1, number):
-        target = peer(step)
-        copy = pltpu.make_async_remote_copy(
-            src_ref=rows_ref.at[target["dp"]],
-            dst_ref=out_ref.at[lax.rem(core + target["dp"], cores), expert],
-            send_sem=send_sem.at[step],
-            recv_sem=recv_sem.at[step],
-            device_id=target,
-            device_id_type=MESH,
+    for way in ways:
+        pl.semaphore_signal(
+            barrier, inc=1, device_id={"expert": index_at(me + way)}, device_id_type=MESH
         )
-        copy.start()
-        copies.append(copy)
+    pl.semaphore_signal(barrier, inc=1, device_id=other, device_id_type=MESH)
+    pl.semaphore_wait(barrier, 3)
+
+    swap = pltpu.make_async_remote_copy(
+        src_ref=rows_ref.at[1 - core],
+        dst_ref=out_ref.at[1, expert],
+        send_sem=swap_sem.at[0],
+        recv_sem=swap_sem.at[1],
+        device_id=other,
+        device_id_type=MESH,
+    )
+    swap.start()
     own = pltpu.make_async_copy(rows_ref.at[core], out_ref.at[0, expert], own_sem)
     own.start()
+
+    most = experts // 2
+    started = {}
+    for hop in range(most):
+        for slot in range(cores):
+            if hop == 0 and slot == 1:
+                swap.wait_recv()
+            for side, way in enumerate(ways):
+                hops = most if side == slot else experts - 1 - most
+                if hop >= hops:
+                    continue
+                if hop > 0:
+                    started[slot, side, hop - 1].wait_recv()
+                block = out_ref.at[slot, index_at(me - way * hop)]
+                copy = pltpu.make_async_remote_copy(
+                    src_ref=rows_ref.at[core] if hop == 0 and slot == 0 else block,
+                    dst_ref=block,
+                    send_sem=send_sem.at[slot, side, hop],
+                    recv_sem=recv_sem.at[slot, side, hop],
+                    device_id={"expert": index_at(me + way)},
+                    device_id_type=MESH,
+                )
+                copy.start()
+                started[slot, side, hop] = copy
     own.wait()
-    for copy in copies:
-        copy.wait()
+    swap.wait_send()
+    for (slot, side, hop), copy in started.items():
+        copy.wait_send()
+        if (slot, side, hop + 1) not in started:
+            copy.wait_recv()
 
 
 def gather(rows, experts):
     cores = rows.shape[0]
-    number = experts * cores
+    steps = (cores, 2, experts // 2)
     return pl.pallas_call(
         functools.partial(gather_kernel, experts, cores),
         out_shape=jax.ShapeDtypeStruct((cores, experts) + rows.shape[1:], rows.dtype),
         in_specs=[pl.BlockSpec(memory_space=pl.ANY)],
         out_specs=pl.BlockSpec(memory_space=pl.ANY),
         scratch_shapes=[
-            pltpu.SemaphoreType.DMA((number,)),
-            pltpu.SemaphoreType.DMA((number,)),
+            pltpu.SemaphoreType.DMA((2,)),
+            pltpu.SemaphoreType.DMA(steps),
+            pltpu.SemaphoreType.DMA(steps),
             pltpu.SemaphoreType.DMA,
         ],
         compiler_params=pltpu.CompilerParams(collective_id=0, has_side_effects=True),
     )(rows)
 
 
-def gram_kernel(factor, left_ref, right_ref, out_ref):
-    total = jnp.dot(left_ref[...], right_ref[...], preferred_element_type=jnp.float32)
+def gram_kernel(factor, rows_ref, mask_ref, right_ref, out_ref):
+    tile, experts, _ = out_ref.shape
+    left = rows_ref[...].astype(jnp.float32)[:, None, :] * mask_ref[...][None, :, :]
+    left = left.reshape(tile * experts, rows_ref.shape[1]).astype(jnp.bfloat16)
+    total = jnp.dot(left, right_ref[...], preferred_element_type=jnp.float32)
     out_ref[...] = (total * factor).reshape(out_ref.shape).astype(out_ref.dtype)
 
 
-def gram(left, right, experts, factor):
-    rows, depth = left.shape
+def gram(rows, mask, right, factor):
+    count, depth = rows.shape
+    experts = mask.shape[0]
     width = right.shape[1]
-    tile = min(64, rows // experts)
+    tile = 64
     return pl.pallas_call(
         functools.partial(gram_kernel, factor),
-        out_shape=jax.ShapeDtypeStruct((rows // experts, experts, width), jnp.bfloat16),
-        grid=(rows // experts // tile,),
+        out_shape=jax.ShapeDtypeStruct((count, experts, width), jnp.bfloat16),
+        grid=(count // tile,),
         in_specs=[
-            pl.BlockSpec((tile * experts, depth), lambda i: (i, 0)),
+            pl.BlockSpec((tile, depth), lambda i: (i, 0)),
+            pl.BlockSpec((experts, depth), lambda i: (0, 0)),
             pl.BlockSpec((depth, width), lambda i: (0, 0)),
         ],
         out_specs=pl.BlockSpec((tile, experts, width), lambda i: (i, 0, 0)),
         compiler_params=pltpu.CompilerParams(vmem_limit_bytes=40 << 20),
         cost_estimate=pl.CostEstimate(
-            flops=2 * rows * depth * width,
-            bytes_accessed=2 * (rows * depth + depth * width + rows * width),
+            flops=2 * count * experts * depth * width,
+            bytes_accessed=2 * (count * depth + depth * width + count * experts * width),
             transcendentals=0,
         ),
-    )(left, right)
+    )(rows, mask, right)
 
 
 def local(tokens, routing, gate_weight, up_weight):
@@ -139,10 +175,7 @@
     mask = jnp.concatenate([own_mask, other_mask], axis=1)
     block = DW // replica_count
     rows = lax.dynamic_slice_in_dim(window, core * block, block, 1).T
-    left = jnp.where(
-        jnp.tile(mask, (block, 1)), jnp.repeat(rows, local_experts, axis=0), jnp.bfloat16(0)
-    )
-    input_gram = gram(left, window, local_experts, factor)
+    input_gram = gram(rows, mask.astype(jnp.float32), window, factor)
 
     hidden_all = jnp.concatenate([hidden, other_hidden], axis=1)
     h_block = hidden_width // replica_count

time: 188 us -> 134 us (0.71)
  the two profiles are of different devices: /device:TPU:13 before, /device:TPU:0 now
where the time goes in v3:
time: 134 us; the launch traced here: 132 us
  Pallas kernels  58.4 us (44%)
  matrix products  44.7 us (33%)
  local copies, waits for them, and re-layouts  13 us (10%)
  starting transfers between devices  7.81 us (6%)
  other arithmetic  7.12 us (5%)
    pallas_call x1, Pallas kernels, gather(): pl.pallas_call(functools.partial(gather_kernel, experts, cores), out_shap...  38.7 us
    dot_general x4, matrix products, project(): return jnp.einsum('td,edh->eth', x, w, preferred_element_type=jnp.float32)  37.5 us
    pallas_call x1, Pallas kernels, gram(): pl.pallas_call(functools.partial(gram_kernel, factor), out_shape=jax.Shap...  19.7 us
    ppermute x2, starting transfers between devices, gathered(): return (x, mask, lax.ppermute(x[:, :DW], 'dp', [(0, 1)]))  7.31 us
    dot_general x1, matrix products, local(): jnp.einsum('eti,etj->iej', h_rows, hidden_all, preferred_element_type=jnp...  7.14 us
    unnamed x17, local copies, waits for them, and re-layouts  6.55 us
  transfers between devices with their start and end apart: 5, of which 0 were waited for; matrix products, arithmetic and copies ran while one was open for 35% of the time, Pallas kernels for 15%

profile of v3, /device:TPU:0, one launch (start us, length us, event | category | flops | bytes accessed | tf_op | source)
XLA Modules:
  0.0 131.8 jit_solution(4894195490750736132)
XLA Ops:
  0.6 0.7 convert.6
  1.3 0.1 copy.16
  1.4 1.0 pad_slice_fusion.1
  2.5 0.8 pad_maximum_fusion.5.rows_ref
  3.3 38.7 %shard_map.59 = bf16[2,8,48,2176]{3,2,1,0:T(8,128)(2,1)} custom-call(bf16[2,48,2176]{2,1,0:T(8,128)(2,1)} %pad_maximum_fusion.5.rows_ref), custom_call_target="tpu_custom_call" | custom-call | tf_op jit(solution)/shard_map/pallas_call | solution.py:81
  42.0 2.2 %fusion.25 = (bf16[1,8,48,2176]{3,2,1,0:T(8,128)(2,1)S(1)}, bf16[1,8,48,2176]{3,2,1,0:T(8,128)(2,1)S(1)}) fusion(bf16[2,8,48,2176]{3,2,1,0:T(8,128)(2,1)} %shard_map.59), kind=kLoop, calls=%fused_computation.47 | loop fusion | bytes 6684672 | tf_op jit(solution)/shard_map/slice | solution.py:159
  44.2 0.0 slice-start
  44.2 0.2 slice.32
  44.4 2.7 %collective-permute-start.1 = (bf16[384,2048]{1,0:T(8,128)(2,1)S(1)}, bf16[384,2048]{1,0:T(8,128)(2,1)}, u32[]{:S(2)}, u32[]{:S(2)}) collective-permute-start(bf16[384,2048]{1,0:T(8,128)(2,1)S(1)} %slice.32), channel_id=1, source_target_pairs={{0,1},{2,3},{4,5},{6,7},{8,9},{10,11},{12,13},{14,15},{16,17},{18,... | collective-permute-start | bytes 4718600 | tf_op jit(solution)/shard_map/ppermute | solution.py:157
  47.2 11.1 %convert_bitcast_fusion = bf16[4,384,768]{2,1,0:T(8,128)(2,1)} fusion(bf16[4,2048,768]{2,1,0:T(8,128)(2,1)} %param.7, bf16[384,2176]{1,0:T(8,128)(2,1)S(1)} %bitcast.45), kind=kOutput, calls=%fused_computation.15 | convolution fusion | flops 4833017856 | bytes 16515072 | tf_op jit(solution)/shard_map/td,edh->eth/dot_general | solution.py:165
  58.3 6.3 %convert_bitcast_fusion.1 = bf16[4,384,768]{2,1,0:T(8,128)(2,1)} fusion(bf16[4,2048,768]{2,1,0:T(8,128)(2,1)S(1)} %bitcast.50, bf16[384,2176]{1,0:T(8,128)(2,1)S(1)} %bitcast.46), kind=kOutput, calls=%fused_computation.16 | convolution fusion | flops 4833017856 | bytes 16515072 | tf_op jit(solution)/shard_map/td,edh->eth/dot_general | solution.py:165
  64.6 0.5 collective-permute-start.2
  65.1 0.7 slice_convert_fusion
  65.9 1.0 copy.18
  66.9 0.1 copy.17
  67.0 0.1 compare_reduce_fusion.1
  67.1 8.2 %fusion.12 = f32[384,4,768]{2,0,1:T(8,128)S(1)} fusion(bf16[4,2048,768]{2,1,0:T(8,128)(2,1)} %param.6, bf16[384,2176]{1,0:T(8,128)(2,1)S(1)} %bitcast.42), kind=kOutput, calls=%fused_computation.22 | convolution fusion | flops 4831838208 | bytes 18874368 | tf_op jit(solution)/shard_map/td,edh->eth/dot_general | solution.py:165
  75.3 0.0 collective-permute-done.1
  75.3 1.4 %broadcast_select_fusion = (bf16[384,2048]{1,0:T(8,128)(2,1)S(1)}, bf16[384,2048]{1,0:T(8,128)(2,1)}) fusion(bf16[384,2048]{1,0:T(8,128)(2,1)} %collective-permute-done.1, pred[]{:T(512)S(6)} %eq.12, bf16[384,2176]{1,0:T(8,128)(2,1)S(1)} %bitcast.48), kind=kLoop, calls=%fused_computation.24 | loop fusion | flops 786432 | bytes 6291457 | tf_op jit(solution)/shard_map/jit(_where)/select_n | solution.py:162
  76.7 4.6 %collective-permute-start = (bf16[384,2048]{1,0:T(8,128)(2,1)}, bf16[384,2048]{1,0:T(8,128)(2,1)}, u32[]{:S(2)}, u32[]{:S(2)}) collective-permute-start(bf16[384,2048]{1,0:T(8,128)(2,1)} %get-tuple-element.13), channel_id=1, source_target_pairs={{0,1},{2,3},{4,5},{6,7},{8,9},{10,11},{12,13},{14,15},{16,17},{18,... | collective-permute-start | bytes 4718600 | tf_op jit(solution)/shard_map/ppermute | solution.py:157
  81.3 0.0 collective-permute-done.3
  81.3 11.9 %fusion.3 = bf16[4,384,768]{2,1,0:T(8,128)(2,1)} fusion(bf16[4,384,768]{2,1,0:T(8,128)(2,1)} %collective-permute-done.3, f32[384,4,768]{2,0,1:T(8,128)S(1)} %fusion.12, bf16[4,384,768]{2,1,0:T(8,128)(2,1)} %collective-permute-done.2, pred[4,384]{1,0:T(4,128)(4,1)S(1)} %get-tuple-element.8, bf16[4,2048,768]{2,1,0:T(8,128)(2,1)} %param.7, ...), kind=kOutput, calls=%fused_computation.7 | convolution fusion | flops 4844814336 | bytes 25953792 | tf_op jit(solution)/shard_map/td,edh->eth/dot_general | solution.py:165
  93.3 0.0 collective-permute-start.4
  93.3 0.2 broadcast_select_fusion.1
  93.5 1.1 copy-done
  94.6 1.3 fusion.8
  95.9 1.8 %copy.19.rows_ref = bf16[1024,768]{1,0:T(8,128)(2,1)S(1)} copy(bf16[1024,768]{0,1:T(8,128)(2,1)} %fusion.8) | data formatting | bytes 3145728 | tf_op jit(solution)/shard_map/transpose | solution.py:177
  97.7 0.0 copy-done.1
  97.8 1.8 %pad_maximum_fusion.2.right_ref = bf16[768,2048]{1,0:T(8,128)(2,1)S(1)} fusion(bf16[384,2048]{1,0:T(8,128)(2,1)} %copy-done.2, bf16[384,2048]{1,0:T(8,128)(2,1)S(1)} %copy-done.1), kind=kLoop, calls=%fused_computation.11 | loop fusion | flops 6291456 | bytes 6291456 | tf_op jit(solution)/shard_map/concatenate | solution.py:174
  99.6 19.7 %shard_map.60 = bf16[1024,4,2048]{2,1,0:T(4,128)(2,1)} custom-call(bf16[1024,768]{1,0:T(8,128)(2,1)S(1)} %copy.19.rows_ref, f32[4,768]{1,0:T(4,128)S(1)} %add_convert_fusion.mask_ref, bf16[768,2048]{1,0:T(8,128)(2,1)S(1)} %pad_maximum_fusion.2.right_ref), custom_call_target="tpu_custom_call" | custom-call | flops 12884901888 | bytes 21495808 | tf_op jit(solution)/shard_map/pallas_call | solution.py:109
  119.3 7.1 %fusion.4 = bf16[384,4,768]{0,2,1:T(8,128)(2,1)} fusion(s32[]{:T(128)S(6)} %select_n.27, bf16[4,384,768]{2,1,0:T(8,128)(2,1)} %fusion.3, bf16[4,384,768]{2,1,0:T(8,128)(2,1)} %collective-permute-done.4), kind=kOutput, calls=%fused_computation.13 | convolution fusion | flops 1828454400 | bytes 11796484 | tf_op jit(solution)/shard_map/eti,etj->iej/dot_general | solution.py:183
  126.5 5.4 %copy.21 = bf16[384,4,768]{2,1,0:T(4,128)(2,1)} copy(bf16[384,4,768]{0,2,1:T(8,128)(2,1)} %fusion.4) | data formatting | bytes 4718592
  (23 shorter events, 0.1 us)
Async XLA Ops:
  44.2 20.9 %copy-start.3 = (bf16[1,8,48,2176]{3,2,1,0:T(8,128)(2,1)}, bf16[1,8,48,2176]{3,2,1,0:T(8,128)(2,1)S(1)}, u32[]{:S(2)}) copy-start(bf16[1,8,48,2176]{3,2,1,0:T(8,128)(2,1)S(1)} %get-tuple-element.11) | copy-start | bytes 5013508
  44.2 14.1 %slice-start = ((s8[12582912]{0:T(1024)(128)(4,1)}), s8[4194304]{0:T(1024)(128)(4,1)S(1)}, s32[]{:S(2)}) async-start(s8[12582912]{0:T(1024)(128)(4,1)} %bitcast.49), calls=%async_computation | async-start | bytes 8388608
  44.4 30.9 %collective-permute-start.1 = (bf16[384,2048]{1,0:T(8,128)(2,1)S(1)}, bf16[384,2048]{1,0:T(8,128)(2,1)}, u32[]{:S(2)}, u32[]{:S(2)}) collective-permute-start(bf16[384,2048]{1,0:T(8,128)(2,1)S(1)} %slice.32), channel_id=1, source_target_pairs={{0,1},{2,3},{4,5},{6,7},{8,9},{10,11},{12,13},{14,15},{16,17},{18,... | collective-permute-start | bytes 4718600 | tf_op jit(solution)/shard_map/ppermute | solution.py:157
  47.2 11.1 %slice-start.1 = ((s8[12582912]{0:T(1024)(128)(4,1)}), s8[4194304]{0:T(1024)(128)(4,1)S(1)}, s32[]{:S(2)}) async-start(s8[12582912]{0:T(1024)(128)(4,1)} %bitcast.49), calls=%async_computation.1 | async-start | bytes 8388608
  47.2 11.2 %slice-start.2 = ((s8[12582912]{0:T(1024)(128)(4,1)}), s8[4194304]{0:T(1024)(128)(4,1)S(1)}, s32[]{:S(2)}) async-start(s8[12582912]{0:T(1024)(128)(4,1)} %bitcast.49), calls=%async_computation.2 | async-start | bytes 8388608
  58.3 23.0 %collective-permute-start.3 = (bf16[4,384,768]{2,1,0:T(8,128)(2,1)}, bf16[4,384,768]{2,1,0:T(8,128)(2,1)}, u32[]{:S(2)}, u32[]{:S(2)}) collective-permute-start(bf16[4,384,768]{2,1,0:T(8,128)(2,1)} %convert_bitcast_fusion), channel_id=1, source_target_pairs={{0,1},{1,0},{2,3},{3,2},{4,5},{5,4},{6,7},{7,6},{8,9},{9,8},{10,11... | collective-permute-start | bytes 7077896 | tf_op jit(solution)/shard_map/ppermute | solution.py:168
  64.6 16.7 %collective-permute-start.2 = (bf16[4,384,768]{2,1,0:T(8,128)(2,1)}, bf16[4,384,768]{2,1,0:T(8,128)(2,1)}, u32[]{:S(2)}, u32[]{:S(2)}) collective-permute-start(bf16[4,384,768]{2,1,0:T(8,128)(2,1)} %convert_bitcast_fusion.1), channel_id=1, source_target_pairs={{0,1},{1,0},{2,3},{3,2},{4,5},{5,4},{6,7},{7,6},{8,9},{9,8},{10,11... | collective-permute-start | bytes 7077896 | tf_op jit(solution)/shard_map/ppermute | solution.py:167
  67.1 8.2 %copy-start.4 = (bf16[1,8,48,2176]{3,2,1,0:T(8,128)(2,1)S(1)}, bf16[1,8,48,2176]{3,2,1,0:T(8,128)(2,1)}, u32[]{:S(2)}) copy-start(bf16[1,8,48,2176]{3,2,1,0:T(8,128)(2,1)} %copy-done.3) | copy-start | bytes 5013508
  76.7 16.7 %copy-start.2 = (bf16[384,2048]{1,0:T(8,128)(2,1)}, bf16[384,2048]{1,0:T(8,128)(2,1)S(1)}, u32[]{:S(2)}) copy-start(bf16[384,2048]{1,0:T(8,128)(2,1)S(1)} %get-tuple-element.12) | copy-start | bytes 4718596
  76.7 16.5 %collective-permute-start = (bf16[384,2048]{1,0:T(8,128)(2,1)}, bf16[384,2048]{1,0:T(8,128)(2,1)}, u32[]{:S(2)}, u32[]{:S(2)}) collective-permute-start(bf16[384,2048]{1,0:T(8,128)(2,1)} %get-tuple-element.13), channel_id=1, source_target_pairs={{0,1},{2,3},{4,5},{6,7},{8,9},{10,11},{12,13},{14,15},{16,17},{18,... | collective-permute-start | bytes 4718600 | tf_op jit(solution)/shard_map/ppermute | solution.py:157
  93.3 26.1 %collective-permute-start.4 = (bf16[4,384,768]{2,1,0:T(8,128)(2,1)}, bf16[4,384,768]{2,1,0:T(8,128)(2,1)}, u32[]{:S(2)}, u32[]{:S(2)}) collective-permute-start(bf16[4,384,768]{2,1,0:T(8,128)(2,1)} %fusion.3), channel_id=1, source_target_pairs={{0,1},{1,0},{2,3},{3,2},{4,5},{5,4},{6,7},{7,6},{8,9},{9,8},{10,11... | collective-permute-start | bytes 7077896 | tf_op jit(solution)/shard_map/ppermute | solution.py:172
  93.5 1.1 copy-start
  95.9 1.9 %copy-start.1 = (bf16[384,2048]{1,0:T(8,128)(2,1)S(1)}, bf16[384,2048]{1,0:T(8,128)(2,1)}, u32[]{:S(2)}) copy-start(bf16[384,2048]{1,0:T(8,128)(2,1)} %copy-done) | copy-start | bytes 4718596

commit v4 on v3

--- a/solution.py
+++ b/solution.py
@@ -12,7 +12,7 @@
 MESH = pl.DeviceIdType.MESH
 
 
-def gather_kernel(experts, cores, rows_ref, out_ref, swap_sem, send_sem, recv_sem, own_sem):
+def gather_kernel(experts, cores, rows_ref, out_ref, twin_ref, swap_sem, send_sem, recv_sem, own_sem, twin_sem):
     expert, core = lax.axis_index("expert"), lax.axis_index("dp")
     other = {"dp": 1 - core}
 
@@ -43,6 +43,20 @@
     swap.start()
     own = pltpu.make_async_copy(rows_ref.at[core], out_ref.at[0, expert], own_sem)
     own.start()
+
+    twins = []
+
+    def hand_over(slot, index):
+        twin = pltpu.make_async_remote_copy(
+            src_ref=out_ref.at[slot, index],
+            dst_ref=twin_ref.at[1 - slot, index],
+            send_sem=twin_sem.at[0, len(twins)],
+            recv_sem=twin_sem.at[1, len(twins)],
+            device_id=other,
+            device_id_type=MESH,
+        )
+        twin.start()
+        twins.append(twin)
 
     most = experts // 2
     started = {}
@@ -56,6 +70,7 @@
                     continue
                 if hop > 0:
                     started[slot, side, hop - 1].wait_recv()
+                    hand_over(slot, index_at(me - way * hop))
                 block = out_ref.at[slot, index_at(me - way * hop)]
                 copy = pltpu.make_async_remote_copy(
                     src_ref=rows_ref.at[core] if hop == 0 and slot == 0 else block,
@@ -68,11 +83,16 @@
                 copy.start()
                 started[slot, side, hop] = copy
     own.wait()
+    hand_over(0, expert)
+    hand_over(1, expert)
     swap.wait_send()
     for (slot, side, hop), copy in started.items():
         copy.wait_send()
         if (slot, side, hop + 1) not in started:
             copy.wait_recv()
+            hand_over(slot, index_at(me - ways[side] * (hop + 1)))
+    for twin in twins:
+        twin.wait()
 
 
 def gather(rows, experts):
@@ -80,14 +100,15 @@
     steps = (cores, 2, experts // 2)
     return pl.pallas_call(
         functools.partial(gather_kernel, experts, cores),
-        out_shape=jax.ShapeDtypeStruct((cores, experts) + rows.shape[1:], rows.dtype),
+        out_shape=[jax.ShapeDtypeStruct((cores, experts) + rows.shape[1:], rows.dtype)] * 2,
         in_specs=[pl.BlockSpec(memory_space=pl.ANY)],
-        out_specs=pl.BlockSpec(memory_space=pl.ANY),
+        out_specs=[pl.BlockSpec(memory_space=pl.ANY)] * 2,
         scratch_shapes=[
             pltpu.SemaphoreType.DMA((2,)),
             pltpu.SemaphoreType.DMA(steps),
             pltpu.SemaphoreType.DMA(steps),
             pltpu.SemaphoreType.DMA,
+            pltpu.SemaphoreType.DMA((2, cores * experts)),
         ],
         compiler_params=pltpu.CompilerParams(collective_id=0, has_side_effects=True),
     )(rows)
@@ -145,21 +166,20 @@
             for c in range(replica_count)
         ]
     )
-    gathered_rows = gather(rows, expert_count)
+    gathered_rows, twin_rows = gather(rows, expert_count)
 
     labels = lax.axis_index("expert") * local_experts + jnp.arange(local_experts)
 
-    def gathered(got):
+    def gathered(got, twin):
         got = got.reshape(expert_count * row_count, got.shape[-1])
+        twin = twin.reshape(got.shape)
         x = got[:, :depth]
         named = got[:, depth : depth + topk].astype(jnp.int32)
         mask = jnp.any(named[None, :, :] == labels[:, None, None], axis=2)
-        return x, mask, lax.ppermute(x[:, :DW], "dp", [(0, 1)])
-
-    own_x, own_mask, sent_own = gathered(gathered_rows[0])
-    other_x, other_mask, sent_other = gathered(gathered_rows[1])
-    own_window = jnp.where(core == 0, own_x[:, :DW], sent_other)
-    other_window = jnp.where(core == 0, other_x[:, :DW], sent_own)
+        return x, mask, jnp.where(core == 0, x[:, :DW], twin[:, :DW])
+
+    own_x, own_mask, own_window = gathered(gathered_rows[0], twin_rows[0])
+    other_x, other_mask, other_window = gathered(gathered_rows[1], twin_rows[1])
 
     def project(x, w):
         return jnp.einsum("td,edh->eth", x, w, preferred_element_type=jnp.float32)

time: 134 us -> 128 us (0.955); the launches traced: 132 us -> 128 us
  starting transfers between devices: 7.81 us -> 0.88 us
  local copies, waits for them, and re-layouts: 13 us -> 14.8 us
  Pallas kernels: 58.4 us -> 60.1 us
    ppermute x2 -> x0, starting transfers between devices: 7.31 us -> none  [gathered(): return (x, mask, lax.ppermute(x[:, :DW], 'dp', [(0, 1)]))]
    slice x2 -> x1, local copies, waits for them, and re-layouts: 2.37 us -> 5.33 us  [local(): other_x, other_mask, other_window = gathered(gathered_rows[1], twin_rows[1])]
    pallas_call x1, Pallas kernels: 38.7 us -> 40.4 us  [gather(): pl.pallas_call(functools.partial(gather_kernel, experts, cores), out_shap...]
    unnamed x17 -> x15, local copies, waits for them, and re-layouts: 6.55 us -> 6.52 us
  transfers between devices with their start and end apart: 5 -> 3, of which waited for: 0 -> 0; matrix products, arithmetic and copies ran while one was open for 35% -> 17% of each run, Pallas kernels for 15% -> 15%
where the time goes in v4:
time: 128 us
  Pallas kernels  60.1 us (47%)
  matrix products  45 us (35%)
  local copies, waits for them, and re-layouts  14.8 us (12%)
  other arithmetic  6.55 us (5%)
    pallas_call x1, Pallas kernels, gather(): pl.pallas_call(functools.partial(gather_kernel, experts, cores), out_shap...  40.4 us
    dot_general x4, matrix products, project(): return jnp.einsum('td,edh->eth', x, w, preferred_element_type=jnp.float32)  37.9 us
    pallas_call x1, Pallas kernels, gram(): pl.pallas_call(functools.partial(gram_kernel, factor), out_shape=jax.Shap...  19.6 us
    dot_general x1, matrix products, local(): jnp.einsum('eti,etj->iej', h_rows, hidden_all, preferred_element_type=jnp...  7.12 us
    unnamed x15, local copies, waits for them, and re-layouts  6.52 us
    slice x1, local copies, waits for them, and re-layouts, local(): other_x, other_mask, other_window = gathered(gathered_rows[1], twin_rows[1])  5.33 us
  transfers between devices with their start and end apart: 3, of which 0 were waited for; matrix products, arithmetic and copies ran while one was open for 17% of the time, Pallas kernels for 15%

profile of v4, /device:TPU:0, one launch (start us, length us, event | category | flops | bytes accessed | tf_op | source)
XLA Modules:
  0.0 128.1 jit_solution(17105848328753058130)
XLA Ops:
  0.6 0.7 convert.6
  1.3 0.1 copy.16
  1.4 1.0 pad_slice_fusion.1
  2.5 0.8 pad_maximum_fusion.5.rows_ref
  3.3 40.4 %shard_map.59 = (bf16[2,8,48,2176]{3,2,1,0:T(8,128)(2,1)}, bf16[2,8,48,2176]{3,2,1,0:T(8,128)(2,1)}) custom-call(bf16[2,48,2176]{2,1,0:T(8,128)(2,1)} %pad_maximum_fusion.5.rows_ref), custom_call_target="tpu_custom_call" | custom-call | tf_op jit(solution)/shard_map/pallas_call | solution.py:101
  43.7 0.0 slice-start
  43.7 5.3 %fusion.25 = (bf16[1,8,48,2176]{3,2,1,0:T(8,128)(2,1)S(1)}, bf16[1,8,48,2176]{3,2,1,0:T(8,128)(2,1)S(1)}, bf16[1,8,48,2176]{3,2,1,0:T(8,128)(2,1)}, bf16[1,8,48,2176]{3,2,1,0:T(8,128)(2,1)}) fusion(bf16[2,8,48,2176]{3,2,1,0:T(8,128)(2,1)} %get-tuple-element.4, bf16[2,8,48,2176]{3,2,1,0:T(8,128)(2,1)} %get-tuple-element.5), kind=kLoop, calls=%fused_computation.47 | loop fusion | bytes 13369344 | tf_op jit(solution)/shard_map/slice | solution.py:182
  49.1 11.5 %convert_bitcast_fusion = bf16[4,384,768]{2,1,0:T(8,128)(2,1)} fusion(bf16[4,2048,768]{2,1,0:T(8,128)(2,1)} %param.7, bf16[384,2176]{1,0:T(8,128)(2,1)S(1)} %bitcast.46), kind=kOutput, calls=%fused_computation.15 | convolution fusion | flops 4833017856 | bytes 16515072 | tf_op jit(solution)/shard_map/td,edh->eth/dot_general | solution.py:185
  60.6 0.4 collective-permute-start.1
  60.9 0.0 slice-done.1
  60.9 6.3 %convert_bitcast_fusion.1 = bf16[4,384,768]{2,1,0:T(8,128)(2,1)} fusion(bf16[4,2048,768]{2,1,0:T(8,128)(2,1)S(1)} %bitcast.53, bf16[384,2176]{1,0:T(8,128)(2,1)S(1)} %bitcast.47), kind=kOutput, calls=%fused_computation.16 | convolution fusion | flops 4833017856 | bytes 16515072 | tf_op jit(solution)/shard_map/td,edh->eth/dot_general | solution.py:185
  67.2 0.1 collective-permute-start
  67.4 0.1 copy.17
  67.5 0.0 copy-done.1
  67.5 0.1 copy.18
  67.6 0.1 compare_reduce_fusion.1
  67.8 8.1 %fusion.12 = f32[384,4,768]{2,0,1:T(8,128)S(1)} fusion(bf16[4,2048,768]{2,1,0:T(8,128)(2,1)} %param.6, bf16[384,2176]{1,0:T(8,128)(2,1)S(1)} %bitcast.43), kind=kOutput, calls=%fused_computation.24 | convolution fusion | flops 4831838208 | bytes 18874368 | tf_op jit(solution)/shard_map/td,edh->eth/dot_general | solution.py:185
  75.8 0.0 collective-permute-done.1
  75.8 0.0 collective-permute-done
  75.8 0.0 copy-start.2
  75.9 12.1 %fusion.3 = bf16[4,384,768]{2,1,0:T(8,128)(2,1)} fusion(bf16[4,384,768]{2,1,0:T(8,128)(2,1)} %collective-permute-done.1, f32[384,4,768]{2,0,1:T(8,128)S(1)} %fusion.12, bf16[4,384,768]{2,1,0:T(8,128)(2,1)} %collective-permute-done, pred[4,384]{1,0:T(4,128)(4,1)S(1)} %get-tuple-element.12, bf16[4,2048,768]{2,1,0:T(8,128)(2,1)} %param.7, ...), kind=kOutput, calls=%fused_computation.7 | convolution fusion | flops 4844814336 | bytes 25953792 | tf_op jit(solution)/shard_map/td,edh->eth/dot_general | solution.py:185
  87.9 0.4 collective-permute-start.2
  88.3 0.2 slice_select_fusion
  88.5 1.6 %slice_select_fusion.1 = bf16[384,2048]{1,0:T(8,128)(2,1)S(1)} fusion(bf16[384,2176]{1,0:T(8,128)(2,1)} %bitcast.50, pred[]{:T(512)S(6)} %eq.12, bf16[384,2176]{1,0:T(8,128)(2,1)S(1)} %bitcast.45), kind=kLoop, calls=%fused_computation.20 | loop fusion | flops 786432 | bytes 4718593 | tf_op jit(solution)/shard_map/jit(_where)/select_n | solution.py:179
  90.1 1.1 copy-done
  91.2 1.3 %fusion.8 = bf16[1024,768]{0,1:T(8,128)(2,1)} fusion(s32[]{:T(128)S(6)} %select_n.25, bf16[384,2048]{1,0:T(8,128)(2,1)S(1)} %slice_select_fusion.1, bf16[384,2048]{1,0:T(8,128)(2,1)S(1)} %slice_select_fusion), kind=kLoop, calls=%fused_computation.18 | loop fusion | flops 3145728 | bytes 4718596 | tf_op jit(solution)/shard_map/transpose | solution.py:197
  92.5 1.7 %copy.19.rows_ref = bf16[1024,768]{1,0:T(8,128)(2,1)S(1)} copy(bf16[1024,768]{0,1:T(8,128)(2,1)} %fusion.8) | data formatting | bytes 3145728 | tf_op jit(solution)/shard_map/transpose | solution.py:197
  94.2 1.8 %pad_maximum_fusion.2.right_ref = bf16[768,2048]{1,0:T(8,128)(2,1)S(1)} fusion(bf16[384,2048]{1,0:T(8,128)(2,1)S(1)} %slice_select_fusion, bf16[384,2048]{1,0:T(8,128)(2,1)} %copy-done), kind=kLoop, calls=%fused_computation.11 | loop fusion | flops 6291456 | bytes 6291456 | tf_op jit(solution)/shard_map/concatenate | solution.py:194
  96.0 19.6 %shard_map.60 = bf16[1024,4,2048]{2,1,0:T(4,128)(2,1)} custom-call(bf16[1024,768]{1,0:T(8,128)(2,1)S(1)} %copy.19.rows_ref, f32[4,768]{1,0:T(4,128)S(1)} %add_convert_fusion.mask_ref, bf16[768,2048]{1,0:T(8,128)(2,1)S(1)} %pad_maximum_fusion.2.right_ref), custom_call_target="tpu_custom_call" | custom-call | flops 12884901888 | bytes 21495808 | tf_op jit(solution)/shard_map/pallas_call | solution.py:130
  115.6 0.0 collective-permute-done.2
  115.6 7.1 %fusion.4 = bf16[384,4,768]{0,2,1:T(8,128)(2,1)} fusion(s32[]{:T(128)S(6)} %select_n.27, bf16[4,384,768]{2,1,0:T(8,128)(2,1)} %fusion.3, bf16[4,384,768]{2,1,0:T(8,128)(2,1)} %collective-permute-done.2), kind=kOutput, calls=%fused_computation.13 | convolution fusion | flops 1828454400 | bytes 11796484 | tf_op jit(solution)/shard_map/eti,etj->iej/dot_general | solution.py:203
  122.8 5.4 %copy.21 = bf16[384,4,768]{2,1,0:T(4,128)(2,1)} copy(bf16[384,4,768]{0,2,1:T(8,128)(2,1)} %fusion.4) | data formatting | bytes 4718592
  (16 shorter events, 0.1 us)
Async XLA Ops:
  43.7 17.2 %slice-start = ((s8[12582912]{0:T(1024)(128)(4,1)}), s8[4194304]{0:T(1024)(128)(4,1)S(1)}, s32[]{:S(2)}) async-start(s8[12582912]{0:T(1024)(128)(4,1)} %bitcast.52), calls=%async_computation | async-start | bytes 8388608
  49.1 18.4 %copy-start.1 = (bf16[1,8,48,2176]{3,2,1,0:T(8,128)(2,1)}, bf16[1,8,48,2176]{3,2,1,0:T(8,128)(2,1)S(1)}, u32[]{:S(2)}) copy-start(bf16[1,8,48,2176]{3,2,1,0:T(8,128)(2,1)S(1)} %get-tuple-element.14) | copy-start | bytes 5013508
  49.1 11.9 %slice-start.1 = ((s8[12582912]{0:T(1024)(128)(4,1)}), s8[4194304]{0:T(1024)(128)(4,1)S(1)}, s32[]{:S(2)}) async-start(s8[12582912]{0:T(1024)(128)(4,1)} %bitcast.52), calls=%async_computation.1 | async-start | bytes 8388608
  49.1 11.9 %slice-start.2 = ((s8[12582912]{0:T(1024)(128)(4,1)}), s8[4194304]{0:T(1024)(128)(4,1)S(1)}, s32[]{:S(2)}) async-start(s8[12582912]{0:T(1024)(128)(4,1)} %bitcast.52), calls=%async_computation.2 | async-start | bytes 8388608
  60.6 15.3 %collective-permute-start.1 = (bf16[4,384,768]{2,1,0:T(8,128)(2,1)}, bf16[4,384,768]{2,1,0:T(8,128)(2,1)}, u32[]{:S(2)}, u32[]{:S(2)}) collective-permute-start(bf16[4,384,768]{2,1,0:T(8,128)(2,1)} %convert_bitcast_fusion), channel_id=1, source_target_pairs={{0,1},{1,0},{2,3},{3,2},{4,5},{5,4},{6,7},{7,6},{8,9},{9,8},{10,11... | collective-permute-start | bytes 7077896 | tf_op jit(solution)/shard_map/ppermute | solution.py:188
  67.2 8.6 %collective-permute-start = (bf16[4,384,768]{2,1,0:T(8,128)(2,1)}, bf16[4,384,768]{2,1,0:T(8,128)(2,1)}, u32[]{:S(2)}, u32[]{:S(2)}) collective-permute-start(bf16[4,384,768]{2,1,0:T(8,128)(2,1)} %convert_bitcast_fusion.1), channel_id=1, source_target_pairs={{0,1},{1,0},{2,3},{3,2},{4,5},{5,4},{6,7},{7,6},{8,9},{9,8},{10,11... | collective-permute-start | bytes 7077896 | tf_op jit(solution)/shard_map/ppermute | solution.py:187
  75.8 12.5 %copy-start.2 = (bf16[1,8,48,2176]{3,2,1,0:T(8,128)(2,1)S(1)}, bf16[1,8,48,2176]{3,2,1,0:T(8,128)(2,1)}, u32[]{:S(2)}) copy-start(bf16[1,8,48,2176]{3,2,1,0:T(8,128)(2,1)} %copy-done.1) | copy-start | bytes 5013508
  75.9 12.5 %copy-start.3 = (bf16[1,8,48,2176]{3,2,1,0:T(8,128)(2,1)S(1)}, bf16[1,8,48,2176]{3,2,1,0:T(8,128)(2,1)}, u32[]{:S(2)}) copy-start(bf16[1,8,48,2176]{3,2,1,0:T(8,128)(2,1)} %get-tuple-element.23) | copy-start | bytes 5013508
  87.9 27.7 %collective-permute-start.2 = (bf16[4,384,768]{2,1,0:T(8,128)(2,1)}, bf16[4,384,768]{2,1,0:T(8,128)(2,1)}, u32[]{:S(2)}, u32[]{:S(2)}) collective-permute-start(bf16[4,384,768]{2,1,0:T(8,128)(2,1)} %fusion.3), channel_id=1, source_target_pairs={{0,1},{1,0},{2,3},{3,2},{4,5},{5,4},{6,7},{7,6},{8,9},{9,8},{10,11... | collective-permute-start | bytes 7077896 | tf_op jit(solution)/shard_map/ppermute | solution.py:192
  90.1 1.1 copy-start
